TPU v7x, 32 devices: a whole 2x2x4 slice. The times are simulated.
32 devices in a mesh: groups: 2 (over x), vec: 16 (over z, y, core).
Axes of the slice: x: 2, y: 2, z: 4, core: 2. Of those that a mesh axis runs over, the one named last changes fastest.
Arguments:
- walkers: bfloat16 [32, 48, 1200], P(('groups', 'vec')), parts along dimension 0, may hold values from -6 to 6, as said below
- points: bfloat16 [2400, 2560], P('groups'), parts along dimension 0, may hold values from -0.1875 to 0.1875
- cholesky: bfloat16 [19200, 2560], P(('groups', 'vec')), parts along dimension 0, may hold values from -1.1953125 to 1.1953125
- field_draws: float32 [32, 9600], P('groups', 'vec'), parts along dimension 0, may hold values from -6 to 6
- counts: int32 [32], P(('groups', 'vec')), parts along dimension 0, may hold values from 0 to 3, as said below
- slot_map: int32 [32], P(('groups', 'vec')), parts along dimension 0, may hold values from 0 to 15, as said below
Outputs:
- walkers_next: bfloat16 [32, 48, 1200], P(('groups', 'vec')), parts along dimension 0
- shifts: float32 [32, 9600], P('groups', 'vec'), parts along dimension 0
There are 2 independent parts, one for each index of `groups`. A program takes and returns all parts, laid end to end along the dimension named above; each array names one. Nothing has to cross between parts.
Inputs may be any that keep to these rules, and one draw needn't show every extreme that they name: The counts sum to 16. `slot_map`: A permutation of the 16 rows. The copies of the walkers of one device (rows k * 1 to k + 1 - 1 of the walkers) land in at most one row of each device. `walkers`: each walker's first 48 columns have diagonal entries in [2, 3] and off-diagonal entries below 1.5 / 48 in magnitude.
All inputs are finite; a program needn't handle non-finite values.
Results may differ from a plain program's by a relative error of at most 0.025.
Values may be sent and summed in bfloat16 or wider, within the bound.
A program may use at most 64 MiB of HBM per device.

v0:
```python
import jax
import jax.numpy as jnp
from jax import lax
from jax.sharding import PartitionSpec as P

ORDER = 4


tau_root = 0.03


def passed_along(value, axis, steps):
    count = lax.axis_size(axis)
    pairs = [(source, (source + steps) % count) for source in range(count)]
    return lax.ppermute(value, axis, pairs)


def green_block(walkers, points):
    electrons = walkers.shape[1]
    square = walkers[:, :, :electrons]
    gram = jnp.einsum("wab,wac->wbc", square, square, preferred_element_type=jnp.float32)
    right_side = jnp.einsum("wab,wam->wbm", square, walkers, preferred_element_type=jnp.float32)
    factor = jnp.linalg.cholesky(gram)
    theta = jax.vmap(lambda lower, rows: jax.scipy.linalg.cho_solve((lower, True), rows))(
        factor, right_side
    )
    projected = jnp.einsum(
        "wam,mp->wap", theta.astype(jnp.bfloat16), points, preferred_element_type=jnp.float32
    )
    return jnp.sum(projected * points[:electrons].astype(jnp.float32)[None], axis=1).astype(
        jnp.bfloat16
    )


def vector_bias(densities, cholesky):
    bias = lax.dot_general(
        densities, cholesky, (((1,), (1,)), ((), ())), preferred_element_type=jnp.float32
    )
    return jnp.clip(bias, -1.0, 1.0)


def propagate_block(walkers, weights, points):
    term_now = walkers
    total = walkers.astype(jnp.float32)
    for order_index in range(1, ORDER + 1):
        projected = jnp.einsum("wem,mp->wep", term_now, points, preferred_element_type=jnp.float32)
        scaled = (projected * weights[:, None, :]).astype(jnp.bfloat16)
        back = (
            jnp.einsum("wep,mp->wem", scaled, points, preferred_element_type=jnp.float32)
            / order_index
        )
        total = total + back
        term_now = back.astype(jnp.bfloat16)
    return total.astype(jnp.bfloat16)


def local(walkers, points, cholesky, field_draws, counts, slot_map):
    loop_size = lax.axis_size("vec")
    my_index = lax.axis_index("vec")
    walk_rows, electrons, orbitals = walkers.shape
    total_rows = field_draws.shape[0]
    densities = green_block(walkers, points)

    def visit_block(position, carried):
        block, partial_value, shift_table = carried
        owner = (my_index - position) % loop_size
        shift_rows = vector_bias(block, cholesky)
        draw_rows = lax.dynamic_slice_in_dim(field_draws, owner * walk_rows, walk_rows, 0)
        field_rows = (draw_rows - shift_rows).astype(jnp.bfloat16)
        partial_value = partial_value + jnp.dot(
            field_rows, cholesky, preferred_element_type=jnp.float32
        )
        shift_table = lax.dynamic_update_slice_in_dim(shift_table, shift_rows, owner * walk_rows, 0)
        block, partial_value = (
            passed_along(block.astype(jnp.float32), "vec", 1).astype(block.dtype),
            passed_along(partial_value, "vec", 1),
        )
        return (block, partial_value, shift_table)

    start_state = (
        densities,
        jnp.zeros(densities.shape, jnp.float32),
        jnp.zeros(field_draws.shape, jnp.float32),
    )
    unused, field_sums, shift_table = lax.fori_loop(0, loop_size, visit_block, start_state)
    weights = tau_root * field_sums
    propagated = propagate_block(walkers, weights, points)
    flat_walkers = propagated.reshape(walk_rows, electrons * orbitals)
    counts_all, slots_all = (
        lax.all_gather(counts, "vec", axis=0, tiled=True),
        lax.all_gather(slot_map, "vec", axis=0, tiled=True),
    )
    ends = jnp.cumsum(counts_all)
    positions = jnp.arange(total_rows, dtype=jnp.int32)
    own_rows = my_index * walk_rows + jnp.arange(walk_rows, dtype=jnp.int32)
    copy_of_row = jnp.sum(
        jnp.where(slots_all[None, :] == own_rows[:, None], positions[None, :], 0), axis=1
    )
    source_row = jnp.sum((ends[None, :] <= copy_of_row[:, None]).astype(jnp.int32), axis=1)
    piece = lax.all_gather(flat_walkers, "vec", axis=0, tiled=True)
    picker = (source_row[:, None] == jnp.arange(piece.shape[0], dtype=jnp.int32)[None, :]).astype(
        jnp.bfloat16
    )
    gathered = jnp.dot(picker, piece, preferred_element_type=jnp.float32)
    walkers_next = gathered.astype(jnp.bfloat16).reshape(walk_rows, electrons, orbitals)
    return (walkers_next, shift_table)


def solution(mesh):
    placed = (
        P(("groups", "vec"), None, None),
        P("groups", None),
        P(("groups", "vec"), None),
        P("groups", "vec"),
        P(("groups", "vec")),
        P(("groups", "vec")),
    )
    return jax.shard_map(
        local,
        mesh=mesh,
        in_specs=placed,
        out_specs=(P(("groups", "vec"), None, None), P("groups", "vec")),
        check_vma=False,
    )
```

profile of v0, /device:TPU:0, one launch (start us, length us, event | category | flops | bytes accessed | tf_op | source)
XLA Modules:
  0.0 242.2 jit_solution(14890336816067850668)
XLA Ops:
  7.2 1.1 fusion.41
  8.3 1.2 fusion.25
  9.6 4.4 %custom-call.11 = f32[1,48,48]{2,1,0:T(8,128)S(1)} custom-call(f32[1,48,48]{2,1,0:T(8,128)S(1)} %fusion.36), custom_call_target="Cholesky" | custom-call | tf_op jit(solution)/shard_map/jit(cholesky)/cholesky | solution.py:23
  15.3 3.7 %custom-call.12 = f32[1,1,48,48]{2,3,1,0:T(8,128)S(1)} custom-call(f32[1,1,48,48]{3,2,1,0:T(8,128)S(1)} %fusion.35), custom_call_target="InvertDiagBlocksLowerTriangular" | custom-call | tf_op jit(solution)/shard_map/vmap(jit(_cho_solve))/triangular_solve | solution.py:24
  19.7 3.9 %fusion.16 = bf16[2560]{0:T(1024)(128)(2,1)S(1)} fusion(bf16[48,1200]{1,0:T(8,128)(2,1)S(1)} %convolution_convert_fusion, bf16[1200,2560]{1,0:T(8,128)(2,1)} %param.9), kind=kOutput, calls=%fused_computation.28 | convolution fusion | flops 295278080 | bytes 6510080 | tf_op jit(solution)/shard_map/wam,mp->wap/dot_general | solution.py:27
  23.7 131.1 %while.19 = (s32[]{:T(128)}, bf16[1,2560]{1,0:T(2,128)(2,1)S(1)}, f32[1,2560]{1,0:T(1,128)S(1)}, f32[16,600]{1,0:T(8,128)S(1)}, s32[]{:T(128)}, /*index=5*/f32[1...) while((s32[]{:T(128)}, bf16[1,2560]{1,0:T(2,128)(2,1)S(1)}, ...), condition=%wide.region_7.8_spmd, body=%wide.region_6.7_spmd.sunk | while | flops 6148377 | bytes 6263392 | solution.py:85
  24.8 1.2 convolution_add_fusion.2
  26.5 2.6 %collective-permute-start = (bf16[1,2560]{1,0:T(2,128)(2,1)S(1)}, bf16[1,2560]{1,0:T(2,128)(2,1)S(1)}, u32[]{:S(2)}, u32[]{:S(2)}) collective-permute-start(bf16[1,2560]{1,0:T(2,128)(2,1)S(1)} %copy.29), channel_id=1, source_target_pairs={{0,1},{1,2},{2,3},{3,4},{4,5},{5,6},{6,7},{7,8},{8,9},{9,10},{10,1... | collective-permute-start | bytes 15368 | tf_op jit(solution)/shard_map/while/body/eval_jaxpr/ppermute | solution.py:15
  29.1 3.8 %collective-permute-done = bf16[1,2560]{1,0:T(2,128)(2,1)S(1)} collective-permute-done((bf16[1,2560]{1,0:T(2,128)(2,1)S(1)}, bf16[1,2560]{1,0:T(2,128)(2,1)S(1)}, u32[]{:S(2)}, u32[]{:S(2)}) %collective-permute-start) | collective-permute-done | bytes 5152 | tf_op jit(solution)/shard_map/while/body/eval_jaxpr/ppermute | solution.py:15
  33.9 1.2 convolution_add_fusion.2
  35.2 5.8 %collective-permute-done = bf16[1,2560]{1,0:T(2,128)(2,1)S(1)} collective-permute-done((bf16[1,2560]{1,0:T(2,128)(2,1)S(1)}, bf16[1,2560]{1,0:T(2,128)(2,1)S(1)}, u32[]{:S(2)}, u32[]{:S(2)}) %collective-permute-start) | collective-permute-done | bytes 5152 | tf_op jit(solution)/shard_map/while/body/eval_jaxpr/ppermute | solution.py:15
  42.0 1.2 convolution_add_fusion.2
  43.4 5.8 %collective-permute-done = bf16[1,2560]{1,0:T(2,128)(2,1)S(1)} collective-permute-done((bf16[1,2560]{1,0:T(2,128)(2,1)S(1)}, bf16[1,2560]{1,0:T(2,128)(2,1)S(1)}, u32[]{:S(2)}, u32[]{:S(2)}) %collective-permute-start) | collective-permute-done | bytes 5152 | tf_op jit(solution)/shard_map/while/body/eval_jaxpr/ppermute | solution.py:15
  50.2 1.2 convolution_add_fusion.2
  51.5 5.8 %collective-permute-done = bf16[1,2560]{1,0:T(2,128)(2,1)S(1)} collective-permute-done((bf16[1,2560]{1,0:T(2,128)(2,1)S(1)}, bf16[1,2560]{1,0:T(2,128)(2,1)S(1)}, u32[]{:S(2)}, u32[]{:S(2)}) %collective-permute-start) | collective-permute-done | bytes 5152 | tf_op jit(solution)/shard_map/while/body/eval_jaxpr/ppermute | solution.py:15
  58.3 1.2 convolution_add_fusion.2
  59.6 5.8 %collective-permute-done = bf16[1,2560]{1,0:T(2,128)(2,1)S(1)} collective-permute-done((bf16[1,2560]{1,0:T(2,128)(2,1)S(1)}, bf16[1,2560]{1,0:T(2,128)(2,1)S(1)}, u32[]{:S(2)}, u32[]{:S(2)}) %collective-permute-start) | collective-permute-done | bytes 5152 | tf_op jit(solution)/shard_map/while/body/eval_jaxpr/ppermute | solution.py:15
  66.4 1.2 convolution_add_fusion.2
  67.8 5.8 %collective-permute-done = bf16[1,2560]{1,0:T(2,128)(2,1)S(1)} collective-permute-done((bf16[1,2560]{1,0:T(2,128)(2,1)S(1)}, bf16[1,2560]{1,0:T(2,128)(2,1)S(1)}, u32[]{:S(2)}, u32[]{:S(2)}) %collective-permute-start) | collective-permute-done | bytes 5152 | tf_op jit(solution)/shard_map/while/body/eval_jaxpr/ppermute | solution.py:15
  74.5 1.2 convolution_add_fusion.2
  75.9 5.8 %collective-permute-done = bf16[1,2560]{1,0:T(2,128)(2,1)S(1)} collective-permute-done((bf16[1,2560]{1,0:T(2,128)(2,1)S(1)}, bf16[1,2560]{1,0:T(2,128)(2,1)S(1)}, u32[]{:S(2)}, u32[]{:S(2)}) %collective-permute-start) | collective-permute-done | bytes 5152 | tf_op jit(solution)/shard_map/while/body/eval_jaxpr/ppermute | solution.py:15
  82.7 1.2 convolution_add_fusion.2
  84.0 5.8 %collective-permute-done = bf16[1,2560]{1,0:T(2,128)(2,1)S(1)} collective-permute-done((bf16[1,2560]{1,0:T(2,128)(2,1)S(1)}, bf16[1,2560]{1,0:T(2,128)(2,1)S(1)}, u32[]{:S(2)}, u32[]{:S(2)}) %collective-permute-start) | collective-permute-done | bytes 5152 | tf_op jit(solution)/shard_map/while/body/eval_jaxpr/ppermute | solution.py:15
  90.8 1.2 convolution_add_fusion.2
  92.2 5.8 %collective-permute-done = bf16[1,2560]{1,0:T(2,128)(2,1)S(1)} collective-permute-done((bf16[1,2560]{1,0:T(2,128)(2,1)S(1)}, bf16[1,2560]{1,0:T(2,128)(2,1)S(1)}, u32[]{:S(2)}, u32[]{:S(2)}) %collective-permute-start) | collective-permute-done | bytes 5152 | tf_op jit(solution)/shard_map/while/body/eval_jaxpr/ppermute | solution.py:15
  98.9 1.2 convolution_add_fusion.2
  100.3 5.8 %collective-permute-done = bf16[1,2560]{1,0:T(2,128)(2,1)S(1)} collective-permute-done((bf16[1,2560]{1,0:T(2,128)(2,1)S(1)}, bf16[1,2560]{1,0:T(2,128)(2,1)S(1)}, u32[]{:S(2)}, u32[]{:S(2)}) %collective-permute-start) | collective-permute-done | bytes 5152 | tf_op jit(solution)/shard_map/while/body/eval_jaxpr/ppermute | solution.py:15
  107.1 1.2 convolution_add_fusion.2
  108.4 5.8 %collective-permute-done = bf16[1,2560]{1,0:T(2,128)(2,1)S(1)} collective-permute-done((bf16[1,2560]{1,0:T(2,128)(2,1)S(1)}, bf16[1,2560]{1,0:T(2,128)(2,1)S(1)}, u32[]{:S(2)}, u32[]{:S(2)}) %collective-permute-start) | collective-permute-done | bytes 5152 | tf_op jit(solution)/shard_map/while/body/eval_jaxpr/ppermute | solution.py:15
  115.2 1.2 convolution_add_fusion.2
  116.6 5.8 %collective-permute-done = bf16[1,2560]{1,0:T(2,128)(2,1)S(1)} collective-permute-done((bf16[1,2560]{1,0:T(2,128)(2,1)S(1)}, bf16[1,2560]{1,0:T(2,128)(2,1)S(1)}, u32[]{:S(2)}, u32[]{:S(2)}) %collective-permute-start) | collective-permute-done | bytes 5152 | tf_op jit(solution)/shard_map/while/body/eval_jaxpr/ppermute | solution.py:15
  123.3 1.2 convolution_add_fusion.2
  124.7 5.8 %collective-permute-done = bf16[1,2560]{1,0:T(2,128)(2,1)S(1)} collective-permute-done((bf16[1,2560]{1,0:T(2,128)(2,1)S(1)}, bf16[1,2560]{1,0:T(2,128)(2,1)S(1)}, u32[]{:S(2)}, u32[]{:S(2)}) %collective-permute-start) | collective-permute-done | bytes 5152 | tf_op jit(solution)/shard_map/while/body/eval_jaxpr/ppermute | solution.py:15
  131.5 1.2 convolution_add_fusion.2
  132.8 5.8 %collective-permute-done = bf16[1,2560]{1,0:T(2,128)(2,1)S(1)} collective-permute-done((bf16[1,2560]{1,0:T(2,128)(2,1)S(1)}, bf16[1,2560]{1,0:T(2,128)(2,1)S(1)}, u32[]{:S(2)}, u32[]{:S(2)}) %collective-permute-start) | collective-permute-done | bytes 5152 | tf_op jit(solution)/shard_map/while/body/eval_jaxpr/ppermute | solution.py:15
  139.6 1.2 convolution_add_fusion.2
  140.9 5.8 %collective-permute-done = bf16[1,2560]{1,0:T(2,128)(2,1)S(1)} collective-permute-done((bf16[1,2560]{1,0:T(2,128)(2,1)S(1)}, bf16[1,2560]{1,0:T(2,128)(2,1)S(1)}, u32[]{:S(2)}, u32[]{:S(2)}) %collective-permute-start) | collective-permute-done | bytes 5152 | tf_op jit(solution)/shard_map/while/body/eval_jaxpr/ppermute | solution.py:15
  147.7 1.2 convolution_add_fusion.2
  149.1 5.8 %collective-permute-done = bf16[1,2560]{1,0:T(2,128)(2,1)S(1)} collective-permute-done((bf16[1,2560]{1,0:T(2,128)(2,1)S(1)}, bf16[1,2560]{1,0:T(2,128)(2,1)S(1)}, u32[]{:S(2)}, u32[]{:S(2)}) %collective-permute-start) | collective-permute-done | bytes 5152 | tf_op jit(solution)/shard_map/while/body/eval_jaxpr/ppermute | solution.py:15
  154.9 7.4 %fusion.20 = f32[48,1200]{1,0:T(8,128)S(1)} fusion(bf16[1200,2560]{1,0:T(8,128)(2,1)} %param.9, f32[2560]{0:T(1024)S(1)} %multiply_reduce_fusion, bf16[1,48,1200]{2,1,0:T(8,128)(2,1)S(1)} %copy-done.1), kind=kOutput, calls=%fused_computation.30 | convolution fusion | flops 590069760 | bytes 6499840 | tf_op jit(solution)/shard_map/wep,mp->wem/dot_general | solution.py:49
  162.3 7.4 %convolution_multiply_fusion.7 = f32[48,1200]{1,0:T(8,128)S(1)} fusion(bf16[1200,2560]{1,0:T(8,128)(2,1)} %param.9, f32[2560]{0:T(1024)S(1)} %multiply_reduce_fusion, f32[48,1200]{1,0:T(8,128)S(1)} %fusion.20), kind=kOutput, calls=%fused_computation.20 | convolution fusion | flops 590184960 | bytes 6615040 | tf_op jit(solution)/shard_map/wep,mp->wem/dot_general | solution.py:49
  169.7 7.4 %convolution_multiply_fusion.6 = f32[48,1200]{1,0:T(8,128)S(1)} fusion(bf16[1200,2560]{1,0:T(8,128)(2,1)} %param.9, f32[2560]{0:T(1024)S(1)} %multiply_reduce_fusion, f32[48,1200]{1,0:T(8,128)S(1)} %convolution_multiply_fusion.7), kind=kOutput, calls=%fused_computation.19 | convolution fusion | flops 590184960 | bytes 6615040 | tf_op jit(solution)/shard_map/wep,mp->wem/dot_general | solution.py:49
  177.1 7.4 %fusion.12 = bf16[1,48,1200]{2,1,0:T(8,128)(2,1)S(1)} fusion(bf16[1200,2560]{1,0:T(8,128)(2,1)} %param.9, f32[48,1200]{1,0:T(8,128)S(1)} %convolution_multiply_fusion.6, f32[48,1200]{1,0:T(8,128)S(1)} %convolution_multiply_fusion.7, f32[48,1200]{1,0:T(8,128)S(1)} %fusion.20, f32[2560]{0:T(1024)S(1)} %multiply_reduce_fusion, ...), kind=kOutput, calls=%fused_computation.23 | convolution fusion | flops 590530560 | bytes 7075840 | tf_op jit(solution)/shard_map/wep,mp->wem/dot_general | solution.py:49
  184.5 1.1 reshape.220
  189.1 7.7 %all-reduce.2 = (s32[16]{0:T(128)S(1)}, s32[16]{0:T(128)S(1)}) all-reduce(s32[16]{0:T(128)S(1)} %dynamic-update-slice.3, s32[16]{0:T(128)S(1)} %dynamic-update-slice.4), channel_id=1, replica_groups=mesh['groups'=2,'vec'=16] {'vec'}, use_global_device_ids=true, to_apply=%add | all-reduce | flops 32 | bytes 256
  197.6 1.3 fusion.48
  198.9 32.2 %all-gather.3.cloned.1.call-done = bf16[16,1,57600]{2,1,0:T(2,128)(2,1)} async-done(((bf16[1,1,57600]{2,1,0:T(2,128)(2,1)}), bf16[16,1,57600]{2,1,0:T(2,128)(2,1)}) %all-gather.3.cloned.1.call-update) | async-done | bytes 1843216 | tf_op jit(solution)/shard_map/all_gather | solution.py:100
  231.1 3.4 %fusion.17 = bf16[57600]{0:T(1024)(128)(2,1)S(1)} fusion(bf16[16,1,57600]{2,1,0:T(2,128)(2,1)} %all-gather.3.cloned.1.call-done, s32[]{:T(128)} %fusion.48), kind=kOutput, calls=%fused_computation.29 | convolution fusion | flops 1843216 | bytes 1958404 | tf_op jit(solution)/shard_map/dot_general | solution.py:104
  (156 shorter events, 22.9 us)
Async XLA Ops:
  7.2 16.6 %copy-start = (bf16[600,2560]{1,0:T(8,128)(2,1)S(1)}, bf16[600,2560]{1,0:T(8,128)(2,1)}, u32[]{:S(2)}) copy-start(bf16[600,2560]{1,0:T(8,128)(2,1)} %param.10) | copy-start | bytes 9216004
  7.2 224.0 %all-gather.3.cloned.1.call-start = ((), (), s32[]{:S(2)}) async-start(), calls=%async_computation | async-start | bytes 3916800 | tf_op jit(solution)/shard_map/all_gather | solution.py:100
  23.7 131.2 %copy-start.1 = (bf16[1,48,1200]{2,1,0:T(8,128)(2,1)S(1)}, bf16[1,48,1200]{2,1,0:T(8,128)(2,1)}, u32[]{:S(2)}) copy-start(bf16[1,48,1200]{2,1,0:T(8,128)(2,1)} %param.8) | copy-start | bytes 345604
  26.0 6.9 %collective-permute-start.1 = (f32[1,2560]{1,0:T(1,128)S(1)}, f32[1,2560]{1,0:T(1,128)S(1)}, u32[]{:S(2)}, u32[]{:S(2)}) collective-permute-start(f32[1,2560]{1,0:T(1,128)S(1)} %convolution_add_fusion.2), channel_id=1, source_target_pairs={{0,1},{1,2},{2,3},{3,4},{4,5},{5,6},{6,7},{7,8},{8,9},{9,10},{10,1... | collective-permute-start | bytes 30728 | tf_op jit(solution)/shard_map/while/body/eval_jaxpr/ppermute | solution.py:15
  26.5 6.5 %collective-permute-start = (bf16[1,2560]{1,0:T(2,128)(2,1)S(1)}, bf16[1,2560]{1,0:T(2,128)(2,1)S(1)}, u32[]{:S(2)}, u32[]{:S(2)}) collective-permute-start(bf16[1,2560]{1,0:T(2,128)(2,1)S(1)} %copy.29), channel_id=1, source_target_pairs={{0,1},{1,2},{2,3},{3,4},{4,5},{5,6},{6,7},{7,8},{8,9},{9,10},{10,1... | collective-permute-start | bytes 15368 | tf_op jit(solution)/shard_map/while/body/eval_jaxpr/ppermute | solution.py:15
  35.1 5.9 %collective-permute-start.1 = (f32[1,2560]{1,0:T(1,128)S(1)}, f32[1,2560]{1,0:T(1,128)S(1)}, u32[]{:S(2)}, u32[]{:S(2)}) collective-permute-start(f32[1,2560]{1,0:T(1,128)S(1)} %convolution_add_fusion.2), channel_id=1, source_target_pairs={{0,1},{1,2},{2,3},{3,4},{4,5},{5,6},{6,7},{7,8},{8,9},{9,10},{10,1... | collective-permute-start | bytes 30728 | tf_op jit(solution)/shard_map/while/body/eval_jaxpr/ppermute | solution.py:15
  35.1 5.9 %collective-permute-start = (bf16[1,2560]{1,0:T(2,128)(2,1)S(1)}, bf16[1,2560]{1,0:T(2,128)(2,1)S(1)}, u32[]{:S(2)}, u32[]{:S(2)}) collective-permute-start(bf16[1,2560]{1,0:T(2,128)(2,1)S(1)} %copy.29), channel_id=1, source_target_pairs={{0,1},{1,2},{2,3},{3,4},{4,5},{5,6},{6,7},{7,8},{8,9},{9,10},{10,1... | collective-permute-start | bytes 15368 | tf_op jit(solution)/shard_map/while/body/eval_jaxpr/ppermute | solution.py:15
  43.3 5.9 %collective-permute-start.1 = (f32[1,2560]{1,0:T(1,128)S(1)}, f32[1,2560]{1,0:T(1,128)S(1)}, u32[]{:S(2)}, u32[]{:S(2)}) collective-permute-start(f32[1,2560]{1,0:T(1,128)S(1)} %convolution_add_fusion.2), channel_id=1, source_target_pairs={{0,1},{1,2},{2,3},{3,4},{4,5},{5,6},{6,7},{7,8},{8,9},{9,10},{10,1... | collective-permute-start | bytes 30728 | tf_op jit(solution)/shard_map/while/body/eval_jaxpr/ppermute | solution.py:15
  43.3 5.9 %collective-permute-start = (bf16[1,2560]{1,0:T(2,128)(2,1)S(1)}, bf16[1,2560]{1,0:T(2,128)(2,1)S(1)}, u32[]{:S(2)}, u32[]{:S(2)}) collective-permute-start(bf16[1,2560]{1,0:T(2,128)(2,1)S(1)} %copy.29), channel_id=1, source_target_pairs={{0,1},{1,2},{2,3},{3,4},{4,5},{5,6},{6,7},{7,8},{8,9},{9,10},{10,1... | collective-permute-start | bytes 15368 | tf_op jit(solution)/shard_map/while/body/eval_jaxpr/ppermute | solution.py:15
  51.4 5.9 %collective-permute-start.1 = (f32[1,2560]{1,0:T(1,128)S(1)}, f32[1,2560]{1,0:T(1,128)S(1)}, u32[]{:S(2)}, u32[]{:S(2)}) collective-permute-start(f32[1,2560]{1,0:T(1,128)S(1)} %convolution_add_fusion.2), channel_id=1, source_target_pairs={{0,1},{1,2},{2,3},{3,4},{4,5},{5,6},{6,7},{7,8},{8,9},{9,10},{10,1... | collective-permute-start | bytes 30728 | tf_op jit(solution)/shard_map/while/body/eval_jaxpr/ppermute | solution.py:15
  51.4 5.9 %collective-permute-start = (bf16[1,2560]{1,0:T(2,128)(2,1)S(1)}, bf16[1,2560]{1,0:T(2,128)(2,1)S(1)}, u32[]{:S(2)}, u32[]{:S(2)}) collective-permute-start(bf16[1,2560]{1,0:T(2,128)(2,1)S(1)} %copy.29), channel_id=1, source_target_pairs={{0,1},{1,2},{2,3},{3,4},{4,5},{5,6},{6,7},{7,8},{8,9},{9,10},{10,1... | collective-permute-start | bytes 15368 | tf_op jit(solution)/shard_map/while/body/eval_jaxpr/ppermute | solution.py:15
  59.5 5.9 %collective-permute-start.1 = (f32[1,2560]{1,0:T(1,128)S(1)}, f32[1,2560]{1,0:T(1,128)S(1)}, u32[]{:S(2)}, u32[]{:S(2)}) collective-permute-start(f32[1,2560]{1,0:T(1,128)S(1)} %convolution_add_fusion.2), channel_id=1, source_target_pairs={{0,1},{1,2},{2,3},{3,4},{4,5},{5,6},{6,7},{7,8},{8,9},{9,10},{10,1... | collective-permute-start | bytes 30728 | tf_op jit(solution)/shard_map/while/body/eval_jaxpr/ppermute | solution.py:15
  59.5 5.9 %collective-permute-start = (bf16[1,2560]{1,0:T(2,128)(2,1)S(1)}, bf16[1,2560]{1,0:T(2,128)(2,1)S(1)}, u32[]{:S(2)}, u32[]{:S(2)}) collective-permute-start(bf16[1,2560]{1,0:T(2,128)(2,1)S(1)} %copy.29), channel_id=1, source_target_pairs={{0,1},{1,2},{2,3},{3,4},{4,5},{5,6},{6,7},{7,8},{8,9},{9,10},{10,1... | collective-permute-start | bytes 15368 | tf_op jit(solution)/shard_map/while/body/eval_jaxpr/ppermute | solution.py:15
  67.7 5.9 %collective-permute-start.1 = (f32[1,2560]{1,0:T(1,128)S(1)}, f32[1,2560]{1,0:T(1,128)S(1)}, u32[]{:S(2)}, u32[]{:S(2)}) collective-permute-start(f32[1,2560]{1,0:T(1,128)S(1)} %convolution_add_fusion.2), channel_id=1, source_target_pairs={{0,1},{1,2},{2,3},{3,4},{4,5},{5,6},{6,7},{7,8},{8,9},{9,10},{10,1... | collective-permute-start | bytes 30728 | tf_op jit(solution)/shard_map/while/body/eval_jaxpr/ppermute | solution.py:15
  67.7 5.9 %collective-permute-start = (bf16[1,2560]{1,0:T(2,128)(2,1)S(1)}, bf16[1,2560]{1,0:T(2,128)(2,1)S(1)}, u32[]{:S(2)}, u32[]{:S(2)}) collective-permute-start(bf16[1,2560]{1,0:T(2,128)(2,1)S(1)} %copy.29), channel_id=1, source_target_pairs={{0,1},{1,2},{2,3},{3,4},{4,5},{5,6},{6,7},{7,8},{8,9},{9,10},{10,1... | collective-permute-start | bytes 15368 | tf_op jit(solution)/shard_map/while/body/eval_jaxpr/ppermute | solution.py:15
  75.8 5.9 %collective-permute-start.1 = (f32[1,2560]{1,0:T(1,128)S(1)}, f32[1,2560]{1,0:T(1,128)S(1)}, u32[]{:S(2)}, u32[]{:S(2)}) collective-permute-start(f32[1,2560]{1,0:T(1,128)S(1)} %convolution_add_fusion.2), channel_id=1, source_target_pairs={{0,1},{1,2},{2,3},{3,4},{4,5},{5,6},{6,7},{7,8},{8,9},{9,10},{10,1... | collective-permute-start | bytes 30728 | tf_op jit(solution)/shard_map/while/body/eval_jaxpr/ppermute | solution.py:15
  75.8 5.9 %collective-permute-start = (bf16[1,2560]{1,0:T(2,128)(2,1)S(1)}, bf16[1,2560]{1,0:T(2,128)(2,1)S(1)}, u32[]{:S(2)}, u32[]{:S(2)}) collective-permute-start(bf16[1,2560]{1,0:T(2,128)(2,1)S(1)} %copy.29), channel_id=1, source_target_pairs={{0,1},{1,2},{2,3},{3,4},{4,5},{5,6},{6,7},{7,8},{8,9},{9,10},{10,1... | collective-permute-start | bytes 15368 | tf_op jit(solution)/shard_map/while/body/eval_jaxpr/ppermute | solution.py:15
  83.9 5.9 %collective-permute-start.1 = (f32[1,2560]{1,0:T(1,128)S(1)}, f32[1,2560]{1,0:T(1,128)S(1)}, u32[]{:S(2)}, u32[]{:S(2)}) collective-permute-start(f32[1,2560]{1,0:T(1,128)S(1)} %convolution_add_fusion.2), channel_id=1, source_target_pairs={{0,1},{1,2},{2,3},{3,4},{4,5},{5,6},{6,7},{7,8},{8,9},{9,10},{10,1... | collective-permute-start | bytes 30728 | tf_op jit(solution)/shard_map/while/body/eval_jaxpr/ppermute | solution.py:15
  83.9 5.9 %collective-permute-start = (bf16[1,2560]{1,0:T(2,128)(2,1)S(1)}, bf16[1,2560]{1,0:T(2,128)(2,1)S(1)}, u32[]{:S(2)}, u32[]{:S(2)}) collective-permute-start(bf16[1,2560]{1,0:T(2,128)(2,1)S(1)} %copy.29), channel_id=1, source_target_pairs={{0,1},{1,2},{2,3},{3,4},{4,5},{5,6},{6,7},{7,8},{8,9},{9,10},{10,1... | collective-permute-start | bytes 15368 | tf_op jit(solution)/shard_map/while/body/eval_jaxpr/ppermute | solution.py:15
  92.0 5.9 %collective-permute-start.1 = (f32[1,2560]{1,0:T(1,128)S(1)}, f32[1,2560]{1,0:T(1,128)S(1)}, u32[]{:S(2)}, u32[]{:S(2)}) collective-permute-start(f32[1,2560]{1,0:T(1,128)S(1)} %convolution_add_fusion.2), channel_id=1, source_target_pairs={{0,1},{1,2},{2,3},{3,4},{4,5},{5,6},{6,7},{7,8},{8,9},{9,10},{10,1... | collective-permute-start | bytes 30728 | tf_op jit(solution)/shard_map/while/body/eval_jaxpr/ppermute | solution.py:15
  92.0 5.9 %collective-permute-start = (bf16[1,2560]{1,0:T(2,128)(2,1)S(1)}, bf16[1,2560]{1,0:T(2,128)(2,1)S(1)}, u32[]{:S(2)}, u32[]{:S(2)}) collective-permute-start(bf16[1,2560]{1,0:T(2,128)(2,1)S(1)} %copy.29), channel_id=1, source_target_pairs={{0,1},{1,2},{2,3},{3,4},{4,5},{5,6},{6,7},{7,8},{8,9},{9,10},{10,1... | collective-permute-start | bytes 15368 | tf_op jit(solution)/shard_map/while/body/eval_jaxpr/ppermute | solution.py:15
  100.2 5.9 %collective-permute-start.1 = (f32[1,2560]{1,0:T(1,128)S(1)}, f32[1,2560]{1,0:T(1,128)S(1)}, u32[]{:S(2)}, u32[]{:S(2)}) collective-permute-start(f32[1,2560]{1,0:T(1,128)S(1)} %convolution_add_fusion.2), channel_id=1, source_target_pairs={{0,1},{1,2},{2,3},{3,4},{4,5},{5,6},{6,7},{7,8},{8,9},{9,10},{10,1... | collective-permute-start | bytes 30728 | tf_op jit(solution)/shard_map/while/body/eval_jaxpr/ppermute | solution.py:15
  100.2 5.9 %collective-permute-start = (bf16[1,2560]{1,0:T(2,128)(2,1)S(1)}, bf16[1,2560]{1,0:T(2,128)(2,1)S(1)}, u32[]{:S(2)}, u32[]{:S(2)}) collective-permute-start(bf16[1,2560]{1,0:T(2,128)(2,1)S(1)} %copy.29), channel_id=1, source_target_pairs={{0,1},{1,2},{2,3},{3,4},{4,5},{5,6},{6,7},{7,8},{8,9},{9,10},{10,1... | collective-permute-start | bytes 15368 | tf_op jit(solution)/shard_map/while/body/eval_jaxpr/ppermute | solution.py:15
  108.3 5.9 %collective-permute-start.1 = (f32[1,2560]{1,0:T(1,128)S(1)}, f32[1,2560]{1,0:T(1,128)S(1)}, u32[]{:S(2)}, u32[]{:S(2)}) collective-permute-start(f32[1,2560]{1,0:T(1,128)S(1)} %convolution_add_fusion.2), channel_id=1, source_target_pairs={{0,1},{1,2},{2,3},{3,4},{4,5},{5,6},{6,7},{7,8},{8,9},{9,10},{10,1... | collective-permute-start | bytes 30728 | tf_op jit(solution)/shard_map/while/body/eval_jaxpr/ppermute | solution.py:15
  108.3 5.9 %collective-permute-start = (bf16[1,2560]{1,0:T(2,128)(2,1)S(1)}, bf16[1,2560]{1,0:T(2,128)(2,1)S(1)}, u32[]{:S(2)}, u32[]{:S(2)}) collective-permute-start(bf16[1,2560]{1,0:T(2,128)(2,1)S(1)} %copy.29), channel_id=1, source_target_pairs={{0,1},{1,2},{2,3},{3,4},{4,5},{5,6},{6,7},{7,8},{8,9},{9,10},{10,1... | collective-permute-start | bytes 15368 | tf_op jit(solution)/shard_map/while/body/eval_jaxpr/ppermute | solution.py:15
  116.4 5.9 %collective-permute-start.1 = (f32[1,2560]{1,0:T(1,128)S(1)}, f32[1,2560]{1,0:T(1,128)S(1)}, u32[]{:S(2)}, u32[]{:S(2)}) collective-permute-start(f32[1,2560]{1,0:T(1,128)S(1)} %convolution_add_fusion.2), channel_id=1, source_target_pairs={{0,1},{1,2},{2,3},{3,4},{4,5},{5,6},{6,7},{7,8},{8,9},{9,10},{10,1... | collective-permute-start | bytes 30728 | tf_op jit(solution)/shard_map/while/body/eval_jaxpr/ppermute | solution.py:15
  116.4 5.9 %collective-permute-start = (bf16[1,2560]{1,0:T(2,128)(2,1)S(1)}, bf16[1,2560]{1,0:T(2,128)(2,1)S(1)}, u32[]{:S(2)}, u32[]{:S(2)}) collective-permute-start(bf16[1,2560]{1,0:T(2,128)(2,1)S(1)} %copy.29), channel_id=1, source_target_pairs={{0,1},{1,2},{2,3},{3,4},{4,5},{5,6},{6,7},{7,8},{8,9},{9,10},{10,1... | collective-permute-start | bytes 15368 | tf_op jit(solution)/shard_map/while/body/eval_jaxpr/ppermute | solution.py:15
  124.6 5.9 %collective-permute-start.1 = (f32[1,2560]{1,0:T(1,128)S(1)}, f32[1,2560]{1,0:T(1,128)S(1)}, u32[]{:S(2)}, u32[]{:S(2)}) collective-permute-start(f32[1,2560]{1,0:T(1,128)S(1)} %convolution_add_fusion.2), channel_id=1, source_target_pairs={{0,1},{1,2},{2,3},{3,4},{4,5},{5,6},{6,7},{7,8},{8,9},{9,10},{10,1... | collective-permute-start | bytes 30728 | tf_op jit(solution)/shard_map/while/body/eval_jaxpr/ppermute | solution.py:15
  124.6 5.9 %collective-permute-start = (bf16[1,2560]{1,0:T(2,128)(2,1)S(1)}, bf16[1,2560]{1,0:T(2,128)(2,1)S(1)}, u32[]{:S(2)}, u32[]{:S(2)}) collective-permute-start(bf16[1,2560]{1,0:T(2,128)(2,1)S(1)} %copy.29), channel_id=1, source_target_pairs={{0,1},{1,2},{2,3},{3,4},{4,5},{5,6},{6,7},{7,8},{8,9},{9,10},{10,1... | collective-permute-start | bytes 15368 | tf_op jit(solution)/shard_map/while/body/eval_jaxpr/ppermute | solution.py:15
  132.7 5.9 %collective-permute-start.1 = (f32[1,2560]{1,0:T(1,128)S(1)}, f32[1,2560]{1,0:T(1,128)S(1)}, u32[]{:S(2)}, u32[]{:S(2)}) collective-permute-start(f32[1,2560]{1,0:T(1,128)S(1)} %convolution_add_fusion.2), channel_id=1, source_target_pairs={{0,1},{1,2},{2,3},{3,4},{4,5},{5,6},{6,7},{7,8},{8,9},{9,10},{10,1... | collective-permute-start | bytes 30728 | tf_op jit(solution)/shard_map/while/body/eval_jaxpr/ppermute | solution.py:15
  132.7 5.9 %collective-permute-start = (bf16[1,2560]{1,0:T(2,128)(2,1)S(1)}, bf16[1,2560]{1,0:T(2,128)(2,1)S(1)}, u32[]{:S(2)}, u32[]{:S(2)}) collective-permute-start(bf16[1,2560]{1,0:T(2,128)(2,1)S(1)} %copy.29), channel_id=1, source_target_pairs={{0,1},{1,2},{2,3},{3,4},{4,5},{5,6},{6,7},{7,8},{8,9},{9,10},{10,1... | collective-permute-start | bytes 15368 | tf_op jit(solution)/shard_map/while/body/eval_jaxpr/ppermute | solution.py:15
  140.8 5.9 %collective-permute-start.1 = (f32[1,2560]{1,0:T(1,128)S(1)}, f32[1,2560]{1,0:T(1,128)S(1)}, u32[]{:S(2)}, u32[]{:S(2)}) collective-permute-start(f32[1,2560]{1,0:T(1,128)S(1)} %convolution_add_fusion.2), channel_id=1, source_target_pairs={{0,1},{1,2},{2,3},{3,4},{4,5},{5,6},{6,7},{7,8},{8,9},{9,10},{10,1... | collective-permute-start | bytes 30728 | tf_op jit(solution)/shard_map/while/body/eval_jaxpr/ppermute | solution.py:15
  140.8 5.9 %collective-permute-start = (bf16[1,2560]{1,0:T(2,128)(2,1)S(1)}, bf16[1,2560]{1,0:T(2,128)(2,1)S(1)}, u32[]{:S(2)}, u32[]{:S(2)}) collective-permute-start(bf16[1,2560]{1,0:T(2,128)(2,1)S(1)} %copy.29), channel_id=1, source_target_pairs={{0,1},{1,2},{2,3},{3,4},{4,5},{5,6},{6,7},{7,8},{8,9},{9,10},{10,1... | collective-permute-start | bytes 15368 | tf_op jit(solution)/shard_map/while/body/eval_jaxpr/ppermute | solution.py:15
  149.0 5.9 %collective-permute-start.1 = (f32[1,2560]{1,0:T(1,128)S(1)}, f32[1,2560]{1,0:T(1,128)S(1)}, u32[]{:S(2)}, u32[]{:S(2)}) collective-permute-start(f32[1,2560]{1,0:T(1,128)S(1)} %convolution_add_fusion.2), channel_id=1, source_target_pairs={{0,1},{1,2},{2,3},{3,4},{4,5},{5,6},{6,7},{7,8},{8,9},{9,10},{10,1... | collective-permute-start | bytes 30728 | tf_op jit(solution)/shard_map/while/body/eval_jaxpr/ppermute | solution.py:15
  149.0 5.9 %collective-permute-start = (bf16[1,2560]{1,0:T(2,128)(2,1)S(1)}, bf16[1,2560]{1,0:T(2,128)(2,1)S(1)}, u32[]{:S(2)}, u32[]{:S(2)}) collective-permute-start(bf16[1,2560]{1,0:T(2,128)(2,1)S(1)} %copy.29), channel_id=1, source_target_pairs={{0,1},{1,2},{2,3},{3,4},{4,5},{5,6},{6,7},{7,8},{8,9},{9,10},{10,1... | collective-permute-start | bytes 15368 | tf_op jit(solution)/shard_map/while/body/eval_jaxpr/ppermute | solution.py:15
  154.9 7.4 %copy-start.2 = (f32[16,600]{1,0:T(8,128)}, f32[16,600]{1,0:T(8,128)S(1)}, u32[]{:S(2)}) copy-start(f32[16,600]{1,0:T(8,128)S(1)} %get-tuple-element.179) | copy-start | bytes 115204
  177.1 9.9 %copy-start.3 = (u32[32]{0:T(128)S(1)}, u32[32]{0:T(128)}, u32[]{:S(2)}) copy-start(u32[32]{0:T(128)} %constant.145) | copy-start | bytes 388
Sparse Core Ops, SparseCore 0:
  185.8 45.2 all-gather.2
where the time goes:
time: 243 us; the launch traced here: 242 us
  waiting for transfers between devices  123 us (51%)
  matrix products  74.1 us (30%)
  between operations  15.5 us (6%)
  other arithmetic  11.6 us (5%)
  blocking collectives  7.68 us (3%)
  local copies, waits for them, and re-layouts  5.6 us (2%)
  starting transfers between devices  3.53 us (1%)
    ppermute x32, waiting for transfers between devices, passed_along(): return lax.ppermute(value, axis, pairs)  90.8 us
    all_gather x1, waiting for transfers between devices, local(): piece = lax.all_gather(flat_walkers, 'vec', axis=0, tiled=True)  32.2 us
    dot_general x4, matrix products, propagate_block(): jnp.einsum('wep,mp->wem', scaled, points, preferred_element_type=jnp.floa...  29.6 us
    dot_general x16, matrix products, visit_block(): jnp.dot(field_rows, cholesky, preferred_element_type=jnp.float32)  19.8 us
    dot_general x16, matrix products, vector_bias(): lax.dot_general(densities, cholesky, (((1,), (1,)), ((), ())), preferred_...  14.4 us
    unnamed x1, blocking collectives  7.68 us
    another operation x3, other arithmetic, green_block(): factor = jnp.linalg.cholesky(gram)  5.05 us
  transfers between devices with their start and end apart: 33, of which 17 were waited for; matrix products, arithmetic and copies ran while one was open for 2% of the time, Pallas kernels for 0%

commit v1 on v0

v1 whole, which is shorter than its diff:
```python
import functools
import math

import jax
import jax.numpy as jnp
from jax import lax
from jax.experimental import pallas as pl
from jax.experimental.pallas import tpu as pltpu
from jax.sharding import PartitionSpec as P

ORDER = 4
TAU_ROOT = 0.03
LANES = 128
ROWS = 16
F32 = jnp.float32
BF16 = jnp.bfloat16
MESH = pl.DeviceIdType.MESH


def dot(a, b):
    return lax.dot_general(a, b, (((1,), (0,)), ((), ())), preferred_element_type=F32)


def dot_nt(a, b):
    return lax.dot_general(a, b, (((1,), (1,)), ((), ())), preferred_element_type=F32)


def dot_tn(a, b):
    return lax.dot_general(a, b, (((0,), (0,)), ((), ())), preferred_element_type=F32)


def split(value):
    high = value.astype(BF16)
    return high, (value - high.astype(F32)).astype(BF16)


def inverse_of(square):
    size = square.shape[0]
    row = lax.broadcasted_iota(jnp.int32, (size, size), 0)
    col = lax.broadcasted_iota(jnp.int32, (size, size), 1)
    eye = row == col
    one = jnp.where(eye, 1.0, 0.0).astype(F32)
    wide = square.astype(F32)
    diagonal = jnp.where(eye, wide, 0.0)
    down = 1.0 / jnp.sum(diagonal, axis=1, keepdims=True)
    across = 1.0 / jnp.sum(diagonal, axis=0, keepdims=True)
    power = jnp.where(eye, 0.0, -wide * down)
    series = one + power
    for _ in range(4):
        low = power.astype(BF16)
        power = dot(low, low)
        series = series + dot(series.astype(BF16), power.astype(BF16))
    guess = series * across
    twice = jnp.concatenate([square, square], axis=1)
    for _ in range(2):
        high, low = split(guess)
        residual = one - dot(twice, jnp.concatenate([high, low], axis=0))
        guess = guess + dot(high, residual.astype(BF16))
    return guess


def kernel(
    sizes,
    counts_ref, slots_ref, walk_ref, draws_ref, points_hbm, chol_hbm,
    out_ref, shift_ref,
    pts, chol, xsend, stash, selected, xrecv, gbar32, gsend, grecv, gwide, gmat,
    psum32, psend, precv, proj, proj_next, scaled, term, total, weight,
    load_sem, a_send, a_recv, b_send, b_recv, c_send, c_recv, d_send, d_recv,
):
    n, tiles, electrons, orbitals, npts, prow = sizes
    me = lax.axis_index("vec")
    group = lax.axis_index("groups")
    row_tiles = electrons // ROWS
    col_tiles = -(-orbitals // LANES)
    pieces = npts // LANES
    width = tiles * LANES
    chunk = math.gcd(npts, 512)

    load_points = pltpu.make_async_copy(points_hbm, pts, load_sem.at[0])
    load_points.start()
    load_chol = pltpu.make_async_copy(chol_hbm, chol, load_sem.at[1])
    load_chol.start()

    barrier = pltpu.get_barrier_semaphore()

    def greet(step, carry):
        pl.semaphore_signal(
            barrier, inc=1, device_id=(group, lax.rem(me + step, n)), device_id_type=MESH
        )
        return carry

    lax.fori_loop(1, n, greet, 0)

    lane = lax.broadcasted_iota(jnp.int32, (ROWS, LANES), 1)
    meta = jnp.where(lane < LANES // 2, counts_ref[0], slots_ref[0]).astype(F32).astype(BF16)
    for relay in range(n):
        for t in range(tiles):
            tile = relay * tiles + t
            if tile < row_tiles * col_tiles:
                r, c = tile // col_tiles, tile % col_tiles
                low, high = c * LANES, min(orbitals, (c + 1) * LANES)
                block = walk_ref[r * ROWS:(r + 1) * ROWS, low:high]
                if high - low < LANES:
                    block = jnp.concatenate(
                        [block, jnp.zeros((ROWS, LANES - (high - low)), BF16)], axis=1
                    )
                xsend[relay, :, t * LANES:(t + 1) * LANES] = block
            else:
                xsend[relay, :, t * LANES:(t + 1) * LANES] = jnp.zeros((ROWS, LANES), BF16)
        xsend[relay, :, width:] = meta

    pl.semaphore_wait(barrier, n - 1)

    def rows_at(index, rows):
        return pl.ds(pl.multiple_of(index * rows, rows), rows)

    def copy_a(step):
        peer = lax.rem(me + step, n)
        return pltpu.make_async_remote_copy(
            src_ref=xsend.at[peer], dst_ref=stash.at[rows_at(me, ROWS)],
            send_sem=a_send.at[step], recv_sem=a_recv.at[step],
            device_id=(group, peer), device_id_type=MESH,
        )

    def copy_b(step):
        peer = lax.rem(me + step, n)
        return pltpu.make_async_remote_copy(
            src_ref=gsend, dst_ref=grecv.at[rows_at(me, prow)],
            send_sem=b_send.at[step], recv_sem=b_recv.at[step],
            device_id=(group, peer), device_id_type=MESH,
        )

    def copy_c(step):
        peer = lax.rem(me + step, n)
        return pltpu.make_async_remote_copy(
            src_ref=psend.at[rows_at(peer, prow)], dst_ref=precv.at[rows_at(me, prow)],
            send_sem=c_send.at[step], recv_sem=c_recv.at[step],
            device_id=(group, peer), device_id_type=MESH,
        )

    def copy_d(step):
        peer = lax.rem(me + step, n)
        return pltpu.make_async_remote_copy(
            src_ref=selected.at[rows_at(peer, ROWS)], dst_ref=xrecv.at[rows_at(me, ROWS)],
            send_sem=d_send.at[step], recv_sem=d_recv.at[step],
            device_id=(group, peer), device_id_type=MESH,
        )

    def start_all(make):
        def body(step, carry):
            make(step).start()
            return carry

        lax.fori_loop(1, n, body, 0)

    def arrived_all(make):
        def body(step, carry):
            make(step).wait_recv()
            return carry

        lax.fori_loop(1, n, body, 0)

    def sent_all(make):
        def body(step, carry):
            make(step).wait_send()
            return carry

        lax.fori_loop(1, n, body, 0)

    start_all(copy_a)
    stash[rows_at(me, ROWS), :] = xsend[me]

    inverse = inverse_of(walk_ref[:, :electrons])
    inv_high, inv_low = split(inverse)
    stacked = jnp.concatenate([inv_high, inv_high, inv_low], axis=1)
    load_points.wait()

    def project(source_ref, target_ref):
        def body(c, carry):
            at = pl.ds(pl.multiple_of(c * chunk, chunk), chunk)
            target_ref[:, at] = dot(source_ref[:, :orbitals], pts[:, at])
            return carry

        lax.fori_loop(0, npts // chunk, body, 0)

    project(walk_ref, proj)
    gbar32[...] = jnp.zeros_like(gbar32)
    for c in range(npts // chunk):
        at = slice(c * chunk, (c + 1) * chunk)
        high, low = split(proj[:, at])
        theta_points = dot(stacked, jnp.concatenate([high, low, high], axis=0))
        density = jnp.sum(
            theta_points * pts[:electrons, at].astype(F32), axis=0, keepdims=True
        )
        for j in range(chunk // LANES):
            k = c * (chunk // LANES) + j
            gbar32[k:k + 1, :] = density[:, j * LANES:(j + 1) * LANES]
    gsend[...] = gbar32[...].astype(BF16)
    start_all(copy_b)
    grecv[rows_at(me, prow), :] = gsend[...]

    arrived_all(copy_a)
    count_rows = stash[:, width:]
    big = n * ROWS
    i0 = lax.broadcasted_iota(jnp.int32, (big, big), 0)
    i1 = lax.broadcasted_iota(jnp.int32, (big, big), 1)
    before = jnp.where((i1 // ROWS <= i0 // ROWS) & (i1 % ROWS == 0), 1.0, 0.0).astype(BF16)
    ends = dot(before, count_rows)[:, :1]
    slot_col = count_rows[:, LANES // 2:LANES // 2 + 1].astype(F32)
    first = i0 % ROWS == 0
    place = (i0 // ROWS).astype(F32)

    wanted = (i1 // ROWS).astype(F32)
    copy_row = jnp.sum(jnp.where(first & (slot_col == wanted), place, 0.0), axis=0, keepdims=True)
    source = jnp.sum(jnp.where(first & (ends <= copy_row), 1.0, 0.0), axis=0, keepdims=True)
    pick = jnp.where((place == source) & (i0 % ROWS == i1 % ROWS), 1.0, 0.0).astype(BF16)
    selected[...] = dot_tn(pick, stash[:, :width]).astype(BF16)
    start_all(copy_d)
    xrecv[rows_at(me, ROWS), :] = selected[rows_at(me, ROWS), :]

    ones = (n, n)
    j1 = lax.broadcasted_iota(jnp.int32, (big, n), 1).astype(F32)
    k0 = lax.broadcasted_iota(jnp.int32, (big, n), 0)
    thin_first = k0 % ROWS == 0
    thin_copy = jnp.sum(
        jnp.where(thin_first & (slot_col == j1), (k0 // ROWS).astype(F32), 0.0),
        axis=0, keepdims=True,
    )
    thin_source = jnp.sum(
        jnp.where(thin_first & (ends <= thin_copy), 1.0, 0.0), axis=0, keepdims=True
    )
    thin_pick = jnp.where(
        lax.broadcasted_iota(jnp.int32, ones, 0).astype(F32) == thin_source, 1.0, 0.0
    ).astype(BF16)

    load_chol.wait()
    arrived_all(copy_b)
    gwide[...] = grecv[...].astype(F32)
    for j in range(pieces):
        gmat[:, j * LANES:(j + 1) * LANES] = gwide[pl.ds(j, n, stride=prow), :].astype(BF16)
    shifts = jnp.clip(dot_nt(gmat[...], chol[...]), -1.0, 1.0)
    shift_ref[...] = shifts
    fields = (draws_ref[...] - shifts).astype(BF16)
    fields = dot_tn(thin_pick, fields).astype(BF16)
    psum32[...] = jnp.zeros_like(psum32)
    for c in range(npts // chunk):
        part = dot(fields, chol[:, c * chunk:(c + 1) * chunk])
        for j in range(chunk // LANES):
            k = c * (chunk // LANES) + j
            psum32[pl.ds(k, n, stride=prow), :] = part[:, j * LANES:(j + 1) * LANES]
    psend[...] = psum32[...].astype(BF16)
    start_all(copy_c)
    own = psum32[rows_at(me, prow), :]

    arrived_all(copy_d)
    for tile in range(row_tiles * col_tiles):
        relay, t = tile // tiles, tile % tiles
        r, c = tile // col_tiles, tile % col_tiles
        low, high = c * LANES, min(orbitals, (c + 1) * LANES)
        block = xrecv[relay * ROWS:(relay + 1) * ROWS, t * LANES:t * LANES + high - low]
        term[r * ROWS:(r + 1) * ROWS, low:high] = block
    total[...] = term[...].astype(F32)
    project(term, proj_next)

    arrived_all(copy_c)
    precv[rows_at(me, prow), :] = jnp.zeros((prow, LANES), BF16)

    def add(w, carry):
        return carry + precv[rows_at(w, prow), :].astype(F32)

    weight[...] = TAU_ROOT * lax.fori_loop(0, n, add, own)

    def scale():
        for j in range(pieces):
            at = slice(j * LANES, (j + 1) * LANES)
            scaled[:, at] = (proj_next[:, at] * weight[j:j + 1, :]).astype(BF16)

    def back(k):
        for low in range(0, orbitals, 256):
            high = min(orbitals, low + 256)
            value = dot_nt(scaled[...], pts[low:high, :]) / k
            total[:, low:high] = total[:, low:high] + value
            term[:, low:high] = value.astype(BF16)

    def taylor(k, carry):
        scale()
        back(k.astype(F32))
        project(term, proj_next)
        return carry

    lax.fori_loop(1, ORDER, taylor, 0)
    scale()
    back(float(ORDER))
    out_ref[...] = total[...].astype(BF16)

    sent_all(copy_a)
    sent_all(copy_b)
    sent_all(copy_c)
    sent_all(copy_d)


def local(walkers, points, cholesky, field_draws, counts, slot_map):
    n = lax.axis_size("vec")
    walk_rows, electrons, orbitals = walkers.shape
    assert walk_rows == 1 and electrons % ROWS == 0
    npts = points.shape[1]
    tile_count = (electrons // ROWS) * (-(-orbitals // LANES))
    tiles = -(-tile_count // n)
    pieces = npts // LANES
    prow = -(-pieces // ROWS) * ROWS
    sizes = (n, tiles, electrons, orbitals, npts, prow)
    width = tiles * LANES
    vmem = pl.BlockSpec(memory_space=pltpu.VMEM)
    smem = pl.BlockSpec(memory_space=pltpu.SMEM)
    hbm = pl.BlockSpec(memory_space=pl.ANY)
    dma = pltpu.SemaphoreType.DMA
    walkers_next, shifts = pl.pallas_call(
        functools.partial(kernel, sizes),
        out_shape=(
            jax.ShapeDtypeStruct((electrons, orbitals), BF16),
            jax.ShapeDtypeStruct(field_draws.shape, F32),
        ),
        in_specs=[smem, smem, vmem, vmem, hbm, hbm],
        out_specs=(vmem, vmem),
        scratch_shapes=[
            pltpu.VMEM(points.shape, BF16),
            pltpu.VMEM(cholesky.shape, BF16),
            pltpu.VMEM((n, ROWS, width + LANES), BF16),
            pltpu.VMEM((n * ROWS, width + LANES), BF16),
            pltpu.VMEM((n * ROWS, width), BF16),
            pltpu.VMEM((n * ROWS, width), BF16),
            pltpu.VMEM((prow, LANES), F32),
            pltpu.VMEM((prow, LANES), BF16),
            pltpu.VMEM((n * prow, LANES), BF16),
            pltpu.VMEM((n * prow, LANES), F32),
            pltpu.VMEM((n, npts), BF16),
            pltpu.VMEM((n * prow, LANES), F32),
            pltpu.VMEM((n * prow, LANES), BF16),
            pltpu.VMEM((n * prow, LANES), BF16),
            pltpu.VMEM((electrons, npts), F32),
            pltpu.VMEM((electrons, npts), F32),
            pltpu.VMEM((electrons, npts), BF16),
            pltpu.VMEM((electrons, orbitals), BF16),
            pltpu.VMEM((electrons, orbitals), F32),
            pltpu.VMEM((prow, LANES), F32),
            dma((2,)),
        ] + [dma((n,))] * 8,
        compiler_params=pltpu.CompilerParams(
            collective_id=0, has_side_effects=True, vmem_limit_bytes=48 * 1024 * 1024
        ),
        cost_estimate=pl.CostEstimate(
            flops=2 * electrons * orbitals * npts * 9 + 4 * cholesky.size * n,
            bytes_accessed=2 * (points.size + cholesky.size),
            transcendentals=0,
        ),
    )(counts, slot_map, walkers[0], field_draws, points, cholesky)
    return walkers_next[None], shifts


def solution(mesh):
    placed = (
        P(("groups", "vec"), None, None),
        P("groups", None),
        P(("groups", "vec"), None),
        P("groups", "vec"),
        P(("groups", "vec")),
        P(("groups", "vec")),
    )
    return jax.shard_map(
        local,
        mesh=mesh,
        in_specs=placed,
        out_specs=(P(("groups", "vec"), None, None), P("groups", "vec")),
        check_vma=False,
    )
```

time: 243 us -> 44.3 us (0.18)
  waiting for transfers between devices: 123 us -> 0 us
  matrix products: 74.1 us -> 0 us
  Pallas kernels: 0 us -> 37.3 us
  between operations: 15.5 us -> 1.94 us
  other arithmetic: 11.6 us -> 0 us
  blocking collectives: 7.68 us -> 0 us
  starting transfers between devices: 3.53 us -> 0 us
    ppermute x32 -> x0, waiting for transfers between devices: 90.8 us -> none  [passed_along(): return lax.ppermute(value, axis, pairs)]
    dot_general x40 -> x0, matrix products: 73.3 us -> none  [the longest x4 29.6 us: propagate_block(): jnp.einsum('wep,mp->wem', scaled, points, preferred_element_type=jnp.floa...]
    pallas_call x0 -> x1, Pallas kernels: none -> 37.3 us  [local(): pl.pallas_call(functools.partial(kernel, sizes), out_shape=(jax.ShapeDtyp...]
    all_gather x1 -> x0, waiting for transfers between devices: 32.2 us -> none  [local(): piece = lax.all_gather(flat_walkers, 'vec', axis=0, tiled=True)]
    another operation x6 -> x0, other arithmetic: 9.57 us -> none  [the longest x3 5.05 us: green_block(): factor = jnp.linalg.cholesky(gram)]
    unnamed x1 -> x0, blocking collectives: 7.68 us -> none
    ppermute x32 -> x0, starting transfers between devices: 3.49 us -> none  [passed_along(): return lax.ppermute(value, axis, pairs)]
  transfers between devices with their start and end apart: 33 -> 0, of which waited for: 17 -> 0; matrix products, arithmetic and copies ran while one was open for 2% -> 0% of each run, Pallas kernels for 0% -> 0%
where the time goes in v1:
time: 44.3 us; the launch traced here: 44.1 us
  Pallas kernels  37.3 us (84%)
  local copies, waits for them, and re-layouts  4.81 us (11%)
  between operations  1.94 us (4%)
    pallas_call x1, Pallas kernels, local(): pl.pallas_call(functools.partial(kernel, sizes), out_shape=(jax.ShapeDtyp...  37.3 us
    unnamed x8, local copies, waits for them, and re-layouts  4.81 us

profile of v1, /device:TPU:0, one launch (start us, length us, event | category | flops | bytes accessed | tf_op | source)
XLA Modules:
  0.0 44.1 jit_solution(1321467140582007321)
XLA Ops:
  1.9 0.0 copy-start
  1.9 1.9 %copy-done = bf16[600,2560]{1,0:T(8,128)(2,1)S(1)} copy-done((bf16[600,2560]{1,0:T(8,128)(2,1)S(1)}, bf16[600,2560]{1,0:T(8,128)(2,1)}, u32[]{:S(2)}) %copy-start) | copy-done | bytes 3072024
  3.8 0.0 copy-start.1
  3.8 0.9 %copy-done.1 = bf16[1,48,1200]{2,1,0:T(8,128)(2,1)S(1)} copy-done((bf16[1,48,1200]{2,1,0:T(8,128)(2,1)S(1)}, bf16[1,48,1200]{2,1,0:T(8,128)(2,1)}, u32[]{:S(2)}) %copy-start.1) | copy-done | bytes 115224
  4.7 0.0 copy-start.2
  4.7 0.8 %copy-done.2 = f32[16,600]{1,0:T(8,128)S(1)} copy-done((f32[16,600]{1,0:T(8,128)S(1)}, f32[16,600]{1,0:T(8,128)}, u32[]{:S(2)}) %copy-start.2) | copy-done | bytes 38424
  5.5 37.3 %shard_map.77 = (bf16[48,1200]{1,0:T(8,128)(2,1)S(1)}, f32[16,600]{1,0:T(8,128)S(1)}) custom-call(s32[1]{0:T(128)S(6)} %copy.10.counts_ref, s32[1]{0:T(128)S(6)} %copy.11.slots_ref, bf16[48,1200]{1,0:T(8,128)(2,1)S(1)} %bitcast.3, f32[16,600]{1,0:T(8,128)S(1)} %copy-done.2, bf16[1200,2560]{1,0:T(8,128)(2,1)} %points_hbm.1, bf16[600,2560]{1,0:T(8,128)(2,1)S(1)} %copy-done), custom_call_target="tpu_custom_call" | custom-call | flops 2752512000 | bytes 9216000 | tf_op jit(solution)/shard_map/pallas_call | solution.py:317
  42.8 0.7 %copy.12 = bf16[1,48,1200]{2,1,0:T(8,128)(2,1)} copy(bf16[1,48,1200]{2,1,0:T(8,128)(2,1)S(1)} %bitcast.2) | data formatting | bytes 230400
  43.4 0.6 %copy.13 = f32[16,600]{1,0:T(8,128)} copy(f32[16,600]{1,0:T(8,128)S(1)} %get-tuple-element.9) | data formatting | bytes 76800
Async XLA Ops:
  1.9 1.9 %copy-start = (bf16[600,2560]{1,0:T(8,128)(2,1)S(1)}, bf16[600,2560]{1,0:T(8,128)(2,1)}, u32[]{:S(2)}) copy-start(bf16[600,2560]{1,0:T(8,128)(2,1)} %chol_hbm.1) | copy-start | bytes 9216004
  3.8 0.9 %copy-start.1 = (bf16[1,48,1200]{2,1,0:T(8,128)(2,1)S(1)}, bf16[1,48,1200]{2,1,0:T(8,128)(2,1)}, u32[]{:S(2)}) copy-start(bf16[1,48,1200]{2,1,0:T(8,128)(2,1)} %param.6) | copy-start | bytes 345604
  4.7 0.8 %copy-start.2 = (f32[16,600]{1,0:T(8,128)S(1)}, f32[16,600]{1,0:T(8,128)}, u32[]{:S(2)}) copy-start(f32[16,600]{1,0:T(8,128)} %draws_ref.1) | copy-start | bytes 115204

commit v2 on v1

v2 whole, which is shorter than its diff:
```python
import functools
import math

import jax
import jax.numpy as jnp
from jax import lax
from jax.experimental import pallas as pl
from jax.experimental.pallas import tpu as pltpu
from jax.sharding import PartitionSpec as P

ORDER = 4
TAU_ROOT = 0.03
LANES = 128
ROWS = 16
F32 = jnp.float32
BF16 = jnp.bfloat16
MESH = pl.DeviceIdType.MESH


def dot(a, b):
    return lax.dot_general(a, b, (((1,), (0,)), ((), ())), preferred_element_type=F32)


def dot_nt(a, b):
    return lax.dot_general(a, b, (((1,), (1,)), ((), ())), preferred_element_type=F32)


def dot_tn(a, b):
    return lax.dot_general(a, b, (((0,), (0,)), ((), ())), preferred_element_type=F32)


def split(value):
    high = value.astype(BF16)
    return high, (value - high.astype(F32)).astype(BF16)


def inverse_of(square):
    size = square.shape[0]
    row = lax.broadcasted_iota(jnp.int32, (size, size), 0)
    col = lax.broadcasted_iota(jnp.int32, (size, size), 1)
    eye = row == col
    one = jnp.where(eye, 1.0, 0.0).astype(F32)
    wide = square.astype(F32)
    diagonal = jnp.where(eye, wide, 0.0)
    down = 1.0 / jnp.sum(diagonal, axis=1, keepdims=True)
    across = 1.0 / jnp.sum(diagonal, axis=0, keepdims=True)
    power = jnp.where(eye, 0.0, -wide * down)
    series = one + power
    for _ in range(4):
        low = power.astype(BF16)
        power = dot(low, low)
        series = series + dot(series.astype(BF16), power.astype(BF16))
    guess = series * across
    twice = jnp.concatenate([square, square], axis=1)
    for _ in range(2):
        high, low = split(guess)
        residual = one - dot(twice, jnp.concatenate([high, low], axis=0))
        guess = guess + dot(high, residual.astype(BF16))
    return guess


def kernel(
    sizes,
    counts_ref, slots_ref, walk_hbm, draws_hbm, points_hbm, chol_hbm,
    out_ref, shift_ref,
    walk, draws, pts, back_pts, chol, xsend, stash, selected, xrecv, gbar32, gsend, grecv, gwide,
    gmat, psum32, psend, precv, proj, scaled, term, total, weight,
    load_sem, points_sem, a_send, a_recv, b_send, b_recv, c_send, c_recv, d_send, d_recv,
):
    n, tiles, electrons, orbitals, npts, prow = sizes
    me = lax.axis_index("vec")
    group = lax.axis_index("groups")
    row_tiles = electrons // ROWS
    col_tiles = -(-orbitals // LANES)
    pieces = npts // LANES
    width = tiles * LANES
    chunk = math.gcd(npts, 512)
    chunks = [slice(low, low + chunk) for low in range(0, npts, chunk)]

    load_walk = pltpu.make_async_copy(walk_hbm.at[0], walk, load_sem.at[0])
    load_walk.start()
    load_points = [
        pltpu.make_async_copy(points_hbm.at[:, at], pts.at[:, at], points_sem.at[c])
        for c, at in enumerate(chunks)
    ]
    for load in load_points:
        load.start()
    load_chol = pltpu.make_async_copy(chol_hbm, chol, load_sem.at[1])
    load_chol.start()
    load_draws = pltpu.make_async_copy(draws_hbm, draws, load_sem.at[2])
    load_draws.start()

    barrier = pltpu.get_barrier_semaphore()

    def greet(step, carry):
        pl.semaphore_signal(
            barrier, inc=1, device_id=(group, lax.rem(me + step, n)), device_id_type=MESH
        )
        return carry

    lax.fori_loop(1, n, greet, 0)

    lane = lax.broadcasted_iota(jnp.int32, (ROWS, LANES), 1)
    meta = jnp.where(lane < LANES // 2, counts_ref[0], slots_ref[0]).astype(F32).astype(BF16)
    load_walk.wait()
    for relay in range(n):
        for t in range(tiles):
            tile = relay * tiles + t
            if tile < row_tiles * col_tiles:
                r, c = tile // col_tiles, tile % col_tiles
                low, high = c * LANES, min(orbitals, (c + 1) * LANES)
                block = walk[r * ROWS:(r + 1) * ROWS, low:high]
                if high - low < LANES:
                    block = jnp.concatenate(
                        [block, jnp.zeros((ROWS, LANES - (high - low)), BF16)], axis=1
                    )
                xsend[relay, :, t * LANES:(t + 1) * LANES] = block
            else:
                xsend[relay, :, t * LANES:(t + 1) * LANES] = jnp.zeros((ROWS, LANES), BF16)
        xsend[relay, :, width:] = meta

    inverse = inverse_of(walk[:, :electrons])
    inv_high, inv_low = split(inverse)
    stacked = jnp.concatenate([inv_high, inv_high, inv_low], axis=1)

    def copies(source, target, send_sem, recv_sem):
        def make(step):
            peer = lax.rem(me + step, n)
            return pltpu.make_async_remote_copy(
                src_ref=source(peer), dst_ref=target.at[me],
                send_sem=send_sem.at[step], recv_sem=recv_sem.at[step],
                device_id=(group, peer), device_id_type=MESH,
            )

        return make

    copy_a = copies(lambda peer: xsend.at[peer], stash, a_send, a_recv)
    copy_b = copies(lambda peer: gsend, grecv, b_send, b_recv)
    copy_c = copies(lambda peer: psend.at[peer], precv, c_send, c_recv)
    copy_d = copies(lambda peer: selected.at[peer], xrecv, d_send, d_recv)

    def each(act):
        def body(step, carry):
            act(step)
            return carry

        lax.fori_loop(1, n, body, 0)

    pl.semaphore_wait(barrier, n - 1)
    each(lambda step: copy_a(step).start())
    stash[me] = xsend[me]

    gbar32[...] = jnp.zeros_like(gbar32)
    for c, at in enumerate(chunks):
        load_points[c].wait()
        high, low = split(dot(walk[...], pts[:, at]))
        theta_points = dot(stacked, jnp.concatenate([high, low, high], axis=0))
        density = jnp.sum(
            theta_points * pts[:electrons, at].astype(F32), axis=0, keepdims=True
        )
        for j in range(chunk // LANES):
            k = c * (chunk // LANES) + j
            gbar32[k:k + 1, :] = density[:, j * LANES:(j + 1) * LANES]
    gsend[...] = gbar32[...].astype(BF16)
    each(lambda step: copy_b(step).start())
    grecv[me] = gsend[...]

    each(lambda step: copy_a(step).wait_recv())
    big = n * ROWS
    shift = ROWS.bit_length() - 1
    held = stash[...].reshape(big, width + LANES)
    count_rows = held[:, width:]
    i0 = lax.broadcasted_iota(jnp.int32, (big, big), 0)
    i1 = lax.broadcasted_iota(jnp.int32, (big, big), 1)
    w0, w1 = i0 >> shift, i1 >> shift
    r0, r1 = i0 & (ROWS - 1), i1 & (ROWS - 1)
    before = jnp.where((w1 <= w0) & (r1 == 0), 1.0, 0.0).astype(BF16)
    ends = dot(before, count_rows)[:, :1]
    slot_col = count_rows[:, LANES // 2:LANES // 2 + 1].astype(F32)
    place = w0.astype(F32)

    def source_of(wanted, first, spot):
        copy_row = jnp.sum(
            jnp.where(first & (slot_col == wanted), spot, 0.0), axis=0, keepdims=True
        )
        return jnp.sum(jnp.where(first & (ends <= copy_row), 1.0, 0.0), axis=0, keepdims=True)

    source = source_of(w1.astype(F32), r0 == 0, place)
    pick = jnp.where((place == source) & (r0 == r1), 1.0, 0.0).astype(BF16)
    chosen = dot_tn(pick, held[:, :width]).astype(BF16)
    selected[...] = chosen.reshape(n, ROWS, width)
    each(lambda step: copy_d(step).start())
    xrecv[me] = selected[me]

    k0 = lax.broadcasted_iota(jnp.int32, (big, n), 0)
    k1 = lax.broadcasted_iota(jnp.int32, (big, n), 1)
    thin = source_of(
        k1.astype(F32), (k0 & (ROWS - 1)) == 0, (k0 >> shift).astype(F32)
    )
    walker_row = lax.broadcasted_iota(jnp.int32, (n, n), 0).astype(F32)
    thin_pick = jnp.where(walker_row == thin, 1.0, 0.0).astype(BF16)

    for at in chunks[:3]:
        back_pts[at, :] = pts[:, at].T

    load_chol.wait()
    load_draws.wait()
    each(lambda step: copy_b(step).wait_recv())
    gwide[...] = grecv[...].astype(F32).reshape(n * prow, LANES)
    for j in range(pieces):
        gmat[:, j * LANES:(j + 1) * LANES] = gwide[pl.ds(j, n, stride=prow), :].astype(BF16)
    shifts = jnp.clip(dot_nt(gmat[...], chol[...]), -1.0, 1.0)
    shift_ref[...] = shifts
    fields = (draws[...] - shifts).astype(BF16)
    fields = dot_tn(thin_pick, fields).astype(BF16)
    psum32[...] = jnp.zeros_like(psum32)
    for c, at in enumerate(chunks):
        part = dot(fields, chol[:, at])
        for j in range(chunk // LANES):
            k = c * (chunk // LANES) + j
            psum32[pl.ds(k, n, stride=prow), :] = part[:, j * LANES:(j + 1) * LANES]
    psend[...] = psum32[...].reshape(n, prow, LANES).astype(BF16)
    each(lambda step: copy_c(step).start())
    precv[me] = psend[me]

    each(lambda step: copy_d(step).wait_recv())
    for tile in range(row_tiles * col_tiles):
        relay, t = tile // tiles, tile % tiles
        r, c = tile // col_tiles, tile % col_tiles
        low, high = c * LANES, min(orbitals, (c + 1) * LANES)
        term[r * ROWS:(r + 1) * ROWS, low:high] = (
            xrecv[relay, :, t * LANES:t * LANES + high - low]
        )
    total[...] = term[...].astype(F32)

    def project():
        for at in chunks:
            proj[:, at] = dot(term[...], pts[:, at])

    def scale():
        for j in range(pieces):
            at = slice(j * LANES, (j + 1) * LANES)
            scaled[:, at] = (proj[:, at] * weight[j:j + 1, :]).astype(BF16)

    def back(k):
        for low in range(0, orbitals, 512):
            high = min(orbitals, low + 512)
            value = dot(scaled[...], back_pts[:, low:high]) / k
            total[:, low:high] = total[:, low:high] + value
            term[:, low:high] = value.astype(BF16)

    project()
    for at in chunks[3:]:
        back_pts[at, :] = pts[:, at].T

    each(lambda step: copy_c(step).wait_recv())
    weight[...] = TAU_ROOT * jnp.sum(precv[...].astype(F32), axis=0)

    def taylor(k, carry):
        scale()
        back(k.astype(F32))
        project()
        return carry

    lax.fori_loop(1, ORDER, taylor, 0)
    scale()
    back(float(ORDER))
    out_ref[0] = total[...].astype(BF16)

    for make in (copy_a, copy_b, copy_c, copy_d):
        each(lambda step: make(step).wait_send())


def local(walkers, points, cholesky, field_draws, counts, slot_map):
    n = lax.axis_size("vec")
    walk_rows, electrons, orbitals = walkers.shape
    assert walk_rows == 1 and electrons % ROWS == 0
    npts = points.shape[1]
    tile_count = (electrons // ROWS) * (-(-orbitals // LANES))
    tiles = -(-tile_count // n)
    pieces = npts // LANES
    prow = -(-pieces // ROWS) * ROWS
    sizes = (n, tiles, electrons, orbitals, npts, prow)
    width = tiles * LANES
    vmem = pl.BlockSpec(memory_space=pltpu.VMEM)
    smem = pl.BlockSpec(memory_space=pltpu.SMEM)
    hbm = pl.BlockSpec(memory_space=pl.ANY)
    dma = pltpu.SemaphoreType.DMA
    f32 = lambda *shape: pltpu.VMEM(shape, F32)
    bf16 = lambda *shape: pltpu.VMEM(shape, BF16)
    return pl.pallas_call(
        functools.partial(kernel, sizes),
        out_shape=(
            jax.ShapeDtypeStruct(walkers.shape, BF16),
            jax.ShapeDtypeStruct(field_draws.shape, F32),
        ),
        in_specs=[smem, smem, hbm, hbm, hbm, hbm],
        out_specs=(vmem, vmem),
        scratch_shapes=[
            bf16(electrons, orbitals),
            f32(*field_draws.shape),
            bf16(*points.shape),
            bf16(npts, orbitals),
            bf16(*cholesky.shape),
            bf16(n, ROWS, width + LANES),
            bf16(n, ROWS, width + LANES),
            bf16(n, ROWS, width),
            bf16(n, ROWS, width),
            f32(prow, LANES),
            bf16(prow, LANES),
            bf16(n, prow, LANES),
            f32(n * prow, LANES),
            bf16(n, npts),
            f32(n * prow, LANES),
            bf16(n, prow, LANES),
            bf16(n, prow, LANES),
            f32(electrons, npts),
            bf16(electrons, npts),
            bf16(electrons, orbitals),
            f32(electrons, orbitals),
            f32(prow, LANES),
            dma((3,)),
            dma((npts // math.gcd(npts, 512),)),
        ] + [dma((n,))] * 8,
        compiler_params=pltpu.CompilerParams(
            collective_id=0, has_side_effects=True, vmem_limit_bytes=60 * 1024 * 1024
        ),
        cost_estimate=pl.CostEstimate(
            flops=2 * electrons * orbitals * npts * 9 + 4 * cholesky.size * n,
            bytes_accessed=2 * (points.size + cholesky.size),
            transcendentals=0,
        ),
    )(counts, slot_map, walkers, field_draws, points, cholesky)


def solution(mesh):
    placed = (
        P(("groups", "vec"), None, None),
        P("groups", None),
        P(("groups", "vec"), None),
        P("groups", "vec"),
        P(("groups", "vec")),
        P(("groups", "vec")),
    )
    return jax.shard_map(
        local,
        mesh=mesh,
        in_specs=placed,
        out_specs=(P(("groups", "vec"), None, None), P("groups", "vec")),
        check_vma=False,
    )
```

time: 44.3 us -> 37.4 us (0.84)
  Pallas kernels: 37.3 us -> 32.3 us
  local copies, waits for them, and re-layouts: 4.81 us -> 2.96 us
    pallas_call x1, Pallas kernels: 37.3 us -> 32.3 us  [local(): pl.pallas_call(functools.partial(kernel, sizes), out_shape=(jax.ShapeDtyp...]
    unnamed x8 -> x2, local copies, waits for them, and re-layouts: 4.81 us -> 2.96 us
where the time goes in v2:
time: 37.4 us; the launch traced here: 37.2 us
  Pallas kernels  32.3 us (86%)
  local copies, waits for them, and re-layouts  2.96 us (8%)
  between operations  1.93 us (5%)
    pallas_call x1, Pallas kernels, local(): pl.pallas_call(functools.partial(kernel, sizes), out_shape=(jax.ShapeDtyp...  32.3 us
    unnamed x2, local copies, waits for them, and re-layouts  2.96 us

profile of v2, /device:TPU:0, one launch (start us, length us, event | category | flops | bytes accessed | tf_op | source)
XLA Modules:
  0.0 37.2 jit_solution(4252668559683871187)
XLA Ops:
  1.9 32.3 %shard_map.77 = (bf16[1,48,1200]{2,1,0:T(8,128)(2,1)}, f32[16,600]{1,0:T(8,128)}) custom-call(s32[1]{0:T(128)S(6)} %copy.10.counts_ref, s32[1]{0:T(128)S(6)} %copy.11.slots_ref, bf16[1,48,1200]{2,1,0:T(8,128)(2,1)} %walk_hbm.1, f32[16,600]{1,0:T(8,128)} %draws_hbm.1, bf16[1200,2560]{1,0:T(8,128)(2,1)} %points_hbm.1, bf16[600,2560]{1,0:T(8,128)(2,1)} %chol_hbm.1), custom_call_target="tpu_custom_call" | custom-call | flops 2752512000 | bytes 9216000 | tf_op jit(solution)/shard_map/pallas_call | solution.py:291
  34.3 1.6 %copy.12 = bf16[1,48,1200]{2,1,0:T(8,128)(2,1)} copy(bf16[1,48,1200]{2,1,0:T(8,128)(2,1)} %get-tuple-element.4) | data formatting | bytes 230400
  35.8 1.4 %copy.13 = f32[16,600]{1,0:T(8,128)} copy(f32[16,600]{1,0:T(8,128)} %get-tuple-element.5) | data formatting | bytes 76800

commit v3 on v2

--- a/solution.py
+++ b/solution.py
@@ -61,11 +61,11 @@
 
 def kernel(
     sizes,
-    counts_ref, slots_ref, walk_hbm, draws_hbm, points_hbm, chol_hbm,
+    counts_hbm, slots_hbm, walk_hbm, draws_hbm, points_hbm, chol_hbm,
     out_ref, shift_ref,
     walk, draws, pts, back_pts, chol, xsend, stash, selected, xrecv, gbar32, gsend, grecv, gwide,
     gmat, psum32, psend, precv, proj, scaled, term, total, weight,
-    load_sem, points_sem, a_send, a_recv, b_send, b_recv, c_send, c_recv, d_send, d_recv,
+    counts_ref, slots_ref, load_sem, points_sem, send_sem, recv_sem,
 ):
     n, tiles, electrons, orbitals, npts, prow = sizes
     me = lax.axis_index("vec")
@@ -79,6 +79,10 @@
 
     load_walk = pltpu.make_async_copy(walk_hbm.at[0], walk, load_sem.at[0])
     load_walk.start()
+    load_counts = pltpu.make_async_copy(counts_hbm, counts_ref, load_sem.at[3])
+    load_counts.start()
+    load_slots = pltpu.make_async_copy(slots_hbm, slots_ref, load_sem.at[4])
+    load_slots.start()
     load_points = [
         pltpu.make_async_copy(points_hbm.at[:, at], pts.at[:, at], points_sem.at[c])
         for c, at in enumerate(chunks)
@@ -98,8 +102,10 @@
         )
         return carry
 
-    lax.fori_loop(1, n, greet, 0)
-
+    lax.fori_loop(1, n, greet, 0, unroll=n <= 16)
+
+    load_counts.wait()
+    load_slots.wait()
     lane = lax.broadcasted_iota(jnp.int32, (ROWS, LANES), 1)
     meta = jnp.where(lane < LANES // 2, counts_ref[0], slots_ref[0]).astype(F32).astype(BF16)
     load_walk.wait()
@@ -119,38 +125,41 @@
                 xsend[relay, :, t * LANES:(t + 1) * LANES] = jnp.zeros((ROWS, LANES), BF16)
         xsend[relay, :, width:] = meta
 
+    class Exchange:
+        def __init__(self, source, target, index):
+            self.source, self.target = source, target
+            self.sems = dict(send_sem=send_sem.at[index], recv_sem=recv_sem.at[index])
+
+        def start(self):
+            def body(step, carry):
+                peer = lax.rem(me + step, n)
+                pltpu.make_async_remote_copy(
+                    src_ref=self.source(peer), dst_ref=self.target.at[me],
+                    device_id=(group, peer), device_id_type=MESH, **self.sems,
+                ).start()
+                return carry
+
+            lax.fori_loop(1, n, body, 0, unroll=n <= 16)
+
+        def all_of_them(self):
+            return pltpu.make_async_remote_copy(
+                src_ref=self.target.at[pl.ds(0, n - 1)], dst_ref=self.target.at[pl.ds(0, n - 1)],
+                device_id=(group, lax.rem(me + 1, n)), device_id_type=MESH, **self.sems,
+            )
+
+    copy_a = Exchange(lambda peer: xsend.at[peer], stash, 0)
+    copy_b = Exchange(lambda peer: gsend, grecv, 1)
+    copy_c = Exchange(lambda peer: psend.at[peer], precv, 2)
+    copy_d = Exchange(lambda peer: selected.at[peer], xrecv, 3)
+
+    pl.semaphore_wait(barrier, n - 1)
+    copy_a.start()
+    stash[me] = xsend[me]
+
     inverse = inverse_of(walk[:, :electrons])
     inv_high, inv_low = split(inverse)
     stacked = jnp.concatenate([inv_high, inv_high, inv_low], axis=1)
 
-    def copies(source, target, send_sem, recv_sem):
-        def make(step):
-            peer = lax.rem(me + step, n)
-            return pltpu.make_async_remote_copy(
-                src_ref=source(peer), dst_ref=target.at[me],
-                send_sem=send_sem.at[step], recv_sem=recv_sem.at[step],
-                device_id=(group, peer), device_id_type=MESH,
-            )
-
-        return make
-
-    copy_a = copies(lambda peer: xsend.at[peer], stash, a_send, a_recv)
-    copy_b = copies(lambda peer: gsend, grecv, b_send, b_recv)
-    copy_c = copies(lambda peer: psend.at[peer], precv, c_send, c_recv)
-    copy_d = copies(lambda peer: selected.at[peer], xrecv, d_send, d_recv)
-
-    def each(act):
-        def body(step, carry):
-            act(step)
-            return carry
-
-        lax.fori_loop(1, n, body, 0)
-
-    pl.semaphore_wait(barrier, n - 1)
-    each(lambda step: copy_a(step).start())
-    stash[me] = xsend[me]
-
-    gbar32[...] = jnp.zeros_like(gbar32)
     for c, at in enumerate(chunks):
         load_points[c].wait()
         high, low = split(dot(walk[...], pts[:, at]))
@@ -162,10 +171,10 @@
             k = c * (chunk // LANES) + j
             gbar32[k:k + 1, :] = density[:, j * LANES:(j + 1) * LANES]
     gsend[...] = gbar32[...].astype(BF16)
-    each(lambda step: copy_b(step).start())
+    copy_b.start()
     grecv[me] = gsend[...]
 
-    each(lambda step: copy_a(step).wait_recv())
+    copy_a.all_of_them().wait_recv()
     big = n * ROWS
     shift = ROWS.bit_length() - 1
     held = stash[...].reshape(big, width + LANES)
@@ -189,8 +198,6 @@
     pick = jnp.where((place == source) & (r0 == r1), 1.0, 0.0).astype(BF16)
     chosen = dot_tn(pick, held[:, :width]).astype(BF16)
     selected[...] = chosen.reshape(n, ROWS, width)
-    each(lambda step: copy_d(step).start())
-    xrecv[me] = selected[me]
 
     k0 = lax.broadcasted_iota(jnp.int32, (big, n), 0)
     k1 = lax.broadcasted_iota(jnp.int32, (big, n), 1)
@@ -205,25 +212,28 @@
 
     load_chol.wait()
     load_draws.wait()
-    each(lambda step: copy_b(step).wait_recv())
-    gwide[...] = grecv[...].astype(F32).reshape(n * prow, LANES)
+    copy_b.all_of_them().wait_recv()
+    copy_d.start()
+    xrecv[me] = selected[me]
+    for w in range(n):
+        gwide[w * prow:w * prow + pieces, :] = grecv[w].astype(F32)
     for j in range(pieces):
         gmat[:, j * LANES:(j + 1) * LANES] = gwide[pl.ds(j, n, stride=prow), :].astype(BF16)
     shifts = jnp.clip(dot_nt(gmat[...], chol[...]), -1.0, 1.0)
     shift_ref[...] = shifts
     fields = (draws[...] - shifts).astype(BF16)
     fields = dot_tn(thin_pick, fields).astype(BF16)
-    psum32[...] = jnp.zeros_like(psum32)
     for c, at in enumerate(chunks):
         part = dot(fields, chol[:, at])
         for j in range(chunk // LANES):
             k = c * (chunk // LANES) + j
             psum32[pl.ds(k, n, stride=prow), :] = part[:, j * LANES:(j + 1) * LANES]
-    psend[...] = psum32[...].reshape(n, prow, LANES).astype(BF16)
-    each(lambda step: copy_c(step).start())
+    for w in range(n):
+        psend[w] = psum32[w * prow:w * prow + pieces, :].astype(BF16)
+    copy_c.start()
     precv[me] = psend[me]
 
-    each(lambda step: copy_d(step).wait_recv())
+    copy_d.all_of_them().wait_recv()
     for tile in range(row_tiles * col_tiles):
         relay, t = tile // tiles, tile % tiles
         r, c = tile // col_tiles, tile % col_tiles
@@ -253,7 +263,7 @@
     for at in chunks[3:]:
         back_pts[at, :] = pts[:, at].T
 
-    each(lambda step: copy_c(step).wait_recv())
+    copy_c.all_of_them().wait_recv()
     weight[...] = TAU_ROOT * jnp.sum(precv[...].astype(F32), axis=0)
 
     def taylor(k, carry):
@@ -267,8 +277,8 @@
     back(float(ORDER))
     out_ref[0] = total[...].astype(BF16)
 
-    for make in (copy_a, copy_b, copy_c, copy_d):
-        each(lambda step: make(step).wait_send())
+    for copy in (copy_a, copy_b, copy_c, copy_d):
+        copy.all_of_them().wait_send()
 
 
 def local(walkers, points, cholesky, field_draws, counts, slot_map):
@@ -279,22 +289,21 @@
     tile_count = (electrons // ROWS) * (-(-orbitals // LANES))
     tiles = -(-tile_count // n)
     pieces = npts // LANES
-    prow = -(-pieces // ROWS) * ROWS
+    prow = -(-pieces // 8) * 8
     sizes = (n, tiles, electrons, orbitals, npts, prow)
     width = tiles * LANES
     vmem = pl.BlockSpec(memory_space=pltpu.VMEM)
-    smem = pl.BlockSpec(memory_space=pltpu.SMEM)
-    hbm = pl.BlockSpec(memory_space=pl.ANY)
+    hbm = pl.BlockSpec(memory_space=pltpu.HBM)
     dma = pltpu.SemaphoreType.DMA
     f32 = lambda *shape: pltpu.VMEM(shape, F32)
     bf16 = lambda *shape: pltpu.VMEM(shape, BF16)
     return pl.pallas_call(
         functools.partial(kernel, sizes),
         out_shape=(
-            jax.ShapeDtypeStruct(walkers.shape, BF16),
-            jax.ShapeDtypeStruct(field_draws.shape, F32),
+            pltpu.VMEM(walkers.shape, BF16),
+            pltpu.VMEM(field_draws.shape, F32),
         ),
-        in_specs=[smem, smem, hbm, hbm, hbm, hbm],
+        in_specs=[hbm, hbm, hbm, hbm, hbm, hbm],
         out_specs=(vmem, vmem),
         scratch_shapes=[
             bf16(electrons, orbitals),
@@ -306,22 +315,26 @@
             bf16(n, ROWS, width + LANES),
             bf16(n, ROWS, width),
             bf16(n, ROWS, width),
-            f32(prow, LANES),
-            bf16(prow, LANES),
-            bf16(n, prow, LANES),
+            f32(pieces, LANES),
+            bf16(pieces, LANES),
+            bf16(n, pieces, LANES),
             f32(n * prow, LANES),
             bf16(n, npts),
             f32(n * prow, LANES),
-            bf16(n, prow, LANES),
-            bf16(n, prow, LANES),
+            bf16(n, pieces, LANES),
+            bf16(n, pieces, LANES),
             f32(electrons, npts),
             bf16(electrons, npts),
             bf16(electrons, orbitals),
             f32(electrons, orbitals),
-            f32(prow, LANES),
-            dma((3,)),
+            f32(pieces, LANES),
+            pltpu.SMEM((1,), jnp.int32),
+            pltpu.SMEM((1,), jnp.int32),
+            dma((5,)),
             dma((npts // math.gcd(npts, 512),)),
-        ] + [dma((n,))] * 8,
+            dma((4,)),
+            dma((4,)),
+        ],
         compiler_params=pltpu.CompilerParams(
             collective_id=0, has_side_effects=True, vmem_limit_bytes=60 * 1024 * 1024
         ),

time: 37.4 us -> 32.9 us (0.88)
  Pallas kernels: 32.3 us -> 29.5 us
  local copies, waits for them, and re-layouts: 2.96 us -> 1.27 us
    pallas_call x1, Pallas kernels: 32.3 us -> 29.5 us  [local(): pl.pallas_call(functools.partial(kernel, sizes), out_shape=(pltpu.VMEM(wa...]
    unnamed x2, local copies, waits for them, and re-layouts: 2.96 us -> 1.27 us
where the time goes in v3:
time: 32.9 us; the launch traced here: 32.7 us
  Pallas kernels  29.5 us (90%)
  between operations  1.93 us (6%)
  local copies, waits for them, and re-layouts  1.27 us (4%)
    pallas_call x1, Pallas kernels, local(): pl.pallas_call(functools.partial(kernel, sizes), out_shape=(pltpu.VMEM(wa...  29.5 us
    unnamed x2, local copies, waits for them, and re-layouts  1.27 us

profile of v3, /device:TPU:0, one launch (start us, length us, event | category | flops | bytes accessed | tf_op | source)
XLA Modules:
  0.0 32.7 jit_solution(7554400609321763703)
XLA Ops:
  1.9 29.5 %shard_map.77 = (bf16[1,48,1200]{2,1,0:T(8,128)(2,1)S(1)}, f32[16,600]{1,0:T(8,128)S(1)}) custom-call(s32[1]{0:T(128)S(6)} %copy.12.counts_hbm, s32[1]{0:T(128)S(6)} %copy.13.slots_hbm, bf16[1,48,1200]{2,1,0:T(8,128)(2,1)} %walk_hbm.1, f32[16,600]{1,0:T(8,128)} %draws_hbm.1, bf16[1200,2560]{1,0:T(8,128)(2,1)} %points_hbm.1, bf16[600,2560]{1,0:T(8,128)(2,1)} %chol_hbm.1), custom_call_target="tpu_custom_call" | custom-call | flops 2752512000 | bytes 9216000 | tf_op jit(solution)/shard_map/pallas_call | solution.py:300
  31.5 0.7 %copy.10 = bf16[1,48,1200]{2,1,0:T(8,128)(2,1)} copy(bf16[1,48,1200]{2,1,0:T(8,128)(2,1)S(1)} %get-tuple-element.2) | data formatting | bytes 230400
  32.1 0.6 %copy.11 = f32[16,600]{1,0:T(8,128)} copy(f32[16,600]{1,0:T(8,128)S(1)} %get-tuple-element.3) | data formatting | bytes 76800

commit v4 on v3

--- a/solution.py
+++ b/solution.py
@@ -132,7 +132,8 @@
 
         def start(self):
             def body(step, carry):
-                peer = lax.rem(me + step, n)
+                far_first = lax.rem(step + n // 2 - 2, n - 1) + 1
+                peer = lax.rem(me + far_first, n)
                 pltpu.make_async_remote_copy(
                     src_ref=self.source(peer), dst_ref=self.target.at[me],
                     device_id=(group, peer), device_id_type=MESH, **self.sems,

time: 32.9 us -> 34.2 us (1.040)
  Pallas kernels: 29.5 us -> 30.9 us
    pallas_call x1, Pallas kernels: 29.5 us -> 30.9 us  [local(): pl.pallas_call(functools.partial(kernel, sizes), out_shape=(pltpu.VMEM(wa...]
where the time goes in v4:
time: 34.2 us; the launch traced here: 34.1 us
  Pallas kernels  30.9 us (90%)
  between operations  1.93 us (6%)
  local copies, waits for them, and re-layouts  1.27 us (4%)
    pallas_call x1, Pallas kernels, local(): pl.pallas_call(functools.partial(kernel, sizes), out_shape=(pltpu.VMEM(wa...  30.9 us
    unnamed x2, local copies, waits for them, and re-layouts  1.27 us

profile of v4, /device:TPU:0, one launch (start us, length us, event | category | flops | bytes accessed | tf_op | source)
XLA Modules:
  0.0 34.1 jit_solution(13454675550237032617)
XLA Ops:
  1.9 30.9 %shard_map.77 = (bf16[1,48,1200]{2,1,0:T(8,128)(2,1)S(1)}, f32[16,600]{1,0:T(8,128)S(1)}) custom-call(s32[1]{0:T(128)S(6)} %copy.12.counts_hbm, s32[1]{0:T(128)S(6)} %copy.13.slots_hbm, bf16[1,48,1200]{2,1,0:T(8,128)(2,1)} %walk_hbm.1, f32[16,600]{1,0:T(8,128)} %draws_hbm.1, bf16[1200,2560]{1,0:T(8,128)(2,1)} %points_hbm.1, bf16[600,2560]{1,0:T(8,128)(2,1)} %chol_hbm.1), custom_call_target="tpu_custom_call" | custom-call | flops 2752512000 | bytes 9216000 | tf_op jit(solution)/shard_map/pallas_call | solution.py:301
  32.8 0.7 %copy.10 = bf16[1,48,1200]{2,1,0:T(8,128)(2,1)} copy(bf16[1,48,1200]{2,1,0:T(8,128)(2,1)S(1)} %get-tuple-element.2) | data formatting | bytes 230400
  33.5 0.6 %copy.11 = f32[16,600]{1,0:T(8,128)} copy(f32[16,600]{1,0:T(8,128)S(1)} %get-tuple-element.3) | data formatting | bytes 76800
